TPU v7x, 32 devices: a whole 2x2x4 slice. The times are simulated.
32 devices in a mesh: grp: 2 (over y), seq: 8 (over z, x), head: 2 (over core).
Axes of the slice: x: 2, y: 2, z: 4, core: 2. Of those that a mesh axis runs over, the one named last changes fastest.
Arguments:
- features: bfloat16 [8192, 2048], P(('grp', 'seq'), 'head'), parts along dimension 0, may hold values from -6 to 6
- keys_proj: bfloat16 [8192, 128], P(('grp', 'seq')), parts along dimension 0, may hold values from -0.5 to 0.5
- query_proj: bfloat16 [8192, 128], P(('grp', 'seq')), parts along dimension 0, may hold values from -0.5 to 0.5
- log_decay: float32 [32, 8192], P('head', ('grp', 'seq')), parts along dimension 1, may hold values from -1 to 0, as said below
- out_weight: bfloat16 [2048, 1024], P(None, 'head'), may hold values from -0.125 to 0.125
- out_grad: bfloat16 [8192, 1024], P(('grp', 'seq'), 'head'), parts along dimension 0, may hold values from -6 to 6
Outputs:
- grad_features: bfloat16 [8192, 2048], P(('grp', 'seq'), 'head'), parts along dimension 0
- grad_proj: float32 [2, 8192, 128], P('head', ('grp', 'seq')), parts along dimension 1
- grad_decay: float32 [32, 8192], P('head', ('grp', 'seq')), parts along dimension 1
There are 2 independent parts, one for each index of `grp`. A program takes and returns all parts, laid end to end along the dimension named above; an argument that names none is the same for every part. Nothing has to cross between parts.
Inputs may be any that keep to these rules, and one draw needn't show every extreme that they name: log_decay is never positive.
All inputs are finite; a program needn't handle non-finite values.
Results may differ from a plain program's by a relative error of at most 0.0049.
Values may be sent and summed in bfloat16 or wider, within the bound.
A program may use at most 192 MiB of HBM per device.

v0:
```python
import jax
import jax.numpy as jnp
from jax import lax
from jax.sharding import PartitionSpec as P

BLOCK = 256


blended = lax.Precision.HIGHEST


def entering(value, axis, join, neutral, backward):
    count, mine = (lax.axis_size(axis), lax.axis_index(axis))
    pieces = jax.tree.map(lambda part: lax.all_gather(part, axis), value)
    if backward:
        pieces = jax.tree.map(lambda part: part[::-1], pieces)
        mine = count - 1 - mine
    running = jax.tree.map(
        lambda part, zero: jnp.full_like(part, 0) + jnp.asarray(zero, part.dtype), value, neutral
    )

    def lap(position, running):
        longer = join(running, jax.tree.map(lambda part: part[position], pieces))
        return jax.tree.map(lambda new, old: jnp.where(position < mine, new, old), longer, running)

    return lax.fori_loop(0, count - 1, lap, running)


def decay_tables(cumulative):
    length = cumulative.shape[-1]
    row_index = lax.broadcasted_iota(jnp.int32, (length, length), 0)
    col_index = lax.broadcasted_iota(jnp.int32, (length, length), 1)
    causal = row_index >= col_index
    log_gap = cumulative[..., :, None] - cumulative[..., None, :]
    within = jnp.where(causal, jnp.exp(jnp.where(causal, log_gap, 0.0)), 0.0)
    tail_decay = jnp.exp(cumulative[..., -1:] - cumulative)
    return (within, tail_decay)


def pair_combine(earlier, nearer):
    return (earlier[0] * nearer[0], nearer[0][:, None, None] * earlier[1] + nearer[1])


def add_terms(first_sum, second_sum):
    return first_sum + second_sum


def body(features, keys_proj, query_proj, log_decay, out_weight, out_grad):
    token_count, inner_width = features.shape
    head_count = log_decay.shape[0]
    head_size = inner_width // head_count
    state_size = keys_proj.shape[1]
    block_count = token_count // BLOCK
    grad_rows = lax.psum_scatter(
        jnp.einsum("kd,td->kt", out_weight, out_grad, preferred_element_type=jnp.float32),
        "head",
        scatter_dimension=0,
        tiled=True,
    )
    grad_output = grad_rows.astype(jnp.bfloat16).reshape(head_count, head_size, block_count, BLOCK)
    feature_blocks = features.reshape(block_count, BLOCK, head_count, head_size)
    key_blocks = keys_proj.reshape(block_count, BLOCK, state_size)
    query_blocks = query_proj.reshape(block_count, BLOCK, state_size)
    cumulative = jnp.cumsum(log_decay.reshape(head_count, block_count, BLOCK), axis=2)
    within, tail_decay = decay_tables(cumulative)
    growth = jnp.exp(cumulative)
    factor = growth[:, :, -1]
    scores = jnp.einsum(
        "kin,kjn->kij", query_blocks, key_blocks, preferred_element_type=jnp.float32
    )
    weights = within * scores[None]
    fresh_state = jnp.einsum(
        "kjhp,hkjn->hkpn",
        feature_blocks,
        tail_decay[..., None] * key_blocks[None],
        precision=blended,
        preferred_element_type=jnp.float32,
    )
    upward = jnp.einsum(
        "hpki,hkin->hkpn",
        grad_output,
        growth[..., None] * query_blocks[None],
        precision=blended,
        preferred_element_type=jnp.float32,
    )
    local_state = jnp.zeros((head_count, head_size, state_size), jnp.float32)
    local_adjoint = jnp.zeros((head_count, head_size, state_size), jnp.float32)
    total_decay = jnp.ones((head_count,), jnp.float32)
    for step_index in range(block_count):
        local_state = factor[:, step_index, None, None] * local_state + fresh_state[:, step_index]
        total_decay = total_decay * factor[:, step_index]
    for step_index in reversed(range(block_count)):
        local_adjoint = upward[:, step_index] + factor[:, step_index, None, None] * local_adjoint
    identity = (
        jnp.ones((head_count,), jnp.float32),
        jnp.zeros((head_count, head_size, state_size), jnp.float32),
    )
    _, state_in = entering((total_decay, local_state), "seq", pair_combine, identity, False)
    _, beyond = entering((total_decay, local_adjoint), "seq", pair_combine, identity, True)
    starts = []
    block_ends = []
    current = state_in
    for step_index in range(block_count):
        starts.append(current)
        current = factor[:, step_index, None, None] * current + fresh_state[:, step_index]
        block_ends.append(current)
    adjoint_list = [None] * block_count
    current = beyond
    for step_index in reversed(range(block_count)):
        adjoint_list[step_index] = current
        current = upward[:, step_index] + factor[:, step_index, None, None] * current
    starts = jnp.stack(starts, axis=1)
    block_ends = jnp.stack(block_ends, axis=1)
    adjoints = jnp.stack(adjoint_list, axis=1)
    local_part = jnp.einsum(
        "hkij,kjhp->hpki",
        weights,
        feature_blocks,
        precision=blended,
        preferred_element_type=jnp.float32,
    )
    carried_part = (
        jnp.einsum(
            "kin,hkpn->hpki",
            query_blocks,
            starts,
            precision=blended,
            preferred_element_type=jnp.float32,
        )
        * growth[:, None]
    )
    outputs = local_part + carried_part
    grad_in = jnp.einsum(
        "hkij,hpki->kjhp",
        weights,
        grad_output,
        precision=blended,
        preferred_element_type=jnp.float32,
    )
    grad_in = (
        grad_in
        + jnp.einsum(
            "kjn,hkpn->kjhp",
            key_blocks,
            adjoints,
            precision=blended,
            preferred_element_type=jnp.float32,
        )
        * jnp.transpose(tail_decay, (1, 2, 0))[..., None]
    )
    mixed_scores = jnp.einsum(
        "hpki,kjhp->hkij", grad_output, feature_blocks, preferred_element_type=jnp.float32
    )
    decayed_mix = within * mixed_scores
    grad_query = jnp.einsum(
        "hkij,kjn->kin",
        decayed_mix,
        key_blocks,
        precision=blended,
        preferred_element_type=jnp.float32,
    )
    grad_query = grad_query + jnp.einsum(
        "hkpn,hpki->kin",
        starts,
        grad_output.astype(jnp.float32) * growth[:, None],
        precision=blended,
        preferred_element_type=jnp.float32,
    )
    grad_keys = jnp.einsum(
        "hkij,kin->kjn",
        decayed_mix,
        query_blocks,
        precision=blended,
        preferred_element_type=jnp.float32,
    )
    grad_keys = grad_keys + jnp.einsum(
        "hkpn,kjhp->kjn",
        adjoints,
        feature_blocks.astype(jnp.float32) * jnp.transpose(tail_decay, (1, 2, 0))[..., None],
        precision=blended,
        preferred_element_type=jnp.float32,
    )
    stacked = jnp.stack(
        [grad_keys.reshape(token_count, state_size), grad_query.reshape(token_count, state_size)]
    )
    grad_proj = lax.psum_scatter(stacked, "head", scatter_dimension=0, tiled=True)
    grad_part = jnp.sum(grad_output.astype(jnp.float32) * outputs, axis=1)
    feat_part = jnp.transpose(
        jnp.sum(feature_blocks.astype(jnp.float32) * grad_in, axis=3), (2, 0, 1)
    )
    mismatch = grad_part - feat_part
    flat_terms = mismatch.reshape(head_count, token_count)
    suffix = jnp.flip(jnp.cumsum(jnp.flip(flat_terms, 1), axis=1), 1)
    later_sum = entering(
        suffix[:, 0], "seq", add_terms, jnp.zeros((head_count,), jnp.float32), True
    )
    grad_decay = suffix + later_sum[:, None]
    grad_features = grad_in.astype(jnp.bfloat16).reshape(token_count, inner_width)
    return (grad_features, grad_proj, grad_decay)


def solution(mesh):
    placed = (
        P(("grp", "seq"), "head"),
        P(("grp", "seq"), None),
        P(("grp", "seq"), None),
        P("head", ("grp", "seq")),
        P(None, "head"),
        P(("grp", "seq"), "head"),
    )
    return jax.shard_map(
        body,
        mesh=mesh,
        in_specs=placed,
        out_specs=(
            P(("grp", "seq"), "head"),
            P("head", ("grp", "seq"), None),
            P("head", ("grp", "seq")),
        ),
        check_vma=False,
    )
```

profile of v0, /device:TPU:0, one launch (start us, length us, event | category | flops | bytes accessed | tf_op | source)
XLA Modules:
  0.0 242.0 jit_solution(5585903865376847833)
XLA Ops:
  8.1 1.5 copy-done
  9.6 4.2 %fusion.51 = f32[2048,512]{1,0:T(8,128)} fusion(bf16[2048,512]{1,0:T(8,128)(2,1)S(1)} %copy-done, bf16[512,512]{1,0:T(8,128)(2,1)} %param.17), kind=kOutput, calls=%fused_computation.89 | convolution fusion | flops 1073741824 | bytes 6815744 | tf_op jit(solution)/shard_map/kd,td->kt/dot_general | solution.py:55
  13.9 1.5 copy.156
  15.5 1.1 reshape.186
  16.6 1.2 reduce-window.14
  18.1 0.2 slice_reduce_fusion.1
  18.4 0.6 dynamic-slice
  19.6 0.2 slice_reduce_fusion.2
  19.9 3.5 %fusion.23 = f32[16,2,64,128]{3,2,1,0:T(8,128)S(1)} fusion(f32[2,256,128]{2,1,0:T(8,128)S(1)} %convert_element_type.35, f32[16,2,256]{2,1,0:T(2,128)S(1)} %copy.163, bf16[2,256,16,64]{1,0,3,2:T(2,128)(2,1)} %reshape.186), kind=kOutput, calls=%fused_computation.34 | convolution fusion | flops 806354944 | bytes 2392064 | tf_op jit(solution)/shard_map/kjhp,hkjn->hkpn/dot_general | solution.py:72
  23.4 1.0 copy-done.4
  24.4 1.0 fusion.41
  25.5 0.7 convert_element_type.31
  26.2 2.5 %reduce-scatter.3.cloned.1.call-done = f32[1024,512]{1,0:T(8,128)} async-done(((f32[2048,512]{1,0:T(8,128)}), f32[1024,512]{1,0:T(8,128)}) %reduce-scatter.3.cloned.1.call-update) | async-done | bytes 2097168 | tf_op jit(solution)/shard_map/reduce_scatter | solution.py:54
  28.8 1.7 convert_element_type.30
  30.5 1.1 reshape.180
  31.6 3.5 %fusion.7 = f32[16,2,64,128]{3,2,1,0:T(8,128)S(1)} fusion(f32[2,256,128]{2,1,0:T(8,128)} %convert_element_type.31, f32[16,2,256]{2,1,0:T(2,128)S(1)} %copy.152, bf16[16,64,2,256]{3,2,1,0:T(2,128)(2,1)} %reshape.180), kind=kOutput, calls=%fused_computation.15 | convolution fusion | flops 806354944 | bytes 2392064 | tf_op jit(solution)/shard_map/hpki,hkin->hkpn/dot_general | solution.py:79
  35.1 1.0 copy-done.3
  36.1 0.9 fusion.42
  37.2 22.2 %all-reduce = f32[128]{0:T(128)S(1)} all-reduce(f32[128]{0:T(128)S(1)} %get-tuple-element.373), channel_id=2, replica_groups=mesh['grp'=2,'seq'=8,'head'=2] {'seq'}, use_global_device_ids=true, to_apply=%add | all-reduce | flops 128 | bytes 1024
  59.5 0.2 fusion.52
  59.8 0.4 copy-done.15
  60.1 0.8 copy-done.13
  60.9 8.6 %fusion.19 = f32[16,2,256,64]{2,3,1,0:T(8,128)} fusion(f32[2,256,256]{2,1,0:T(8,128)S(1)} %fusion.52, f32[16,2,256]{2,1,0:T(2,128)S(1)} %copy.148, pred[256,256]{1,0:T(8,128)(4,1)S(1)} %iota_compare_fusion, bf16[2,256,16,64]{1,0,3,2:T(2,128)(2,1)} %reshape.186), kind=kOutput, calls=%fused_computation.33 | convolution fusion | flops 1619001344 | bytes 3768320 | tf_op jit(solution)/shard_map/hkij,kjhp->hpki/dot_general | solution.py:115
  69.5 32.0 %all-gather.7.cloned.1.call-done = f32[8,16,64,128]{3,2,1,0:T(8,128)} async-done(((f32[1,16,64,128]{3,2,1,0:T(8,128)}), f32[8,16,64,128]{3,2,1,0:T(8,128)}) %all-gather.7.cloned.1.call-update) | async-done | bytes 4194320 | tf_op jit(solution)/shard_map/all_gather | solution.py:14
  101.5 8.5 %while.43 = (s32[]{:T(128)}, f32[16,64,128]{2,1,0:T(8,128)S(1)}, s32[]{:T(128)}, f32[8,16]{1,0:T(8,128)S(1)}, f32[8,16,64,128]{3,2,1,0:T(8,128)}, /*index=5*/s32[]{:T(128)}, s32[]{:T(128)}) while((s32[]{:T(128)}, f32[16,64,128]{2,1,0:T(8,128)S(1)}, s32[]{:T(128)}, f32[8,16]{1,0:T(8,128)S(1)}, f32[8,16,64,128]{3,2,1,0:T(8,128)}, ...), condition=%wide.region_7.8_spmd.clone, body=%wide.region_6.7_spmd.clone.sunk | while | flops 524292 | bytes 1573169 | solution.py:26
  101.5 1.2 fusion.69
  102.7 1.2 fusion.69
  103.9 1.2 fusion.69
  105.1 1.2 fusion.69
  106.4 1.2 fusion.69
  107.6 1.2 fusion.69
  108.8 1.2 fusion.69
  110.0 1.3 fusion.43
  111.4 4.7 %fusion.26 = f32[2,256,128]{2,1,0:T(8,128)S(1)} fusion(f32[16,2,256]{2,1,0:T(2,128)S(1)} %copy.152, bf16[16,64,2,256]{3,2,1,0:T(2,128)(2,1)} %reshape.180, f32[16,1,64,128]{3,2,0,1:T(8,128)S(1)} %fusion.43, f32[16,1,64,128]{3,2,0,1:T(8,128)S(1)} %bitcast.148), kind=kOutput, calls=%fused_computation.37 | convolution fusion | flops 806617088 | bytes 2392064 | tf_op jit(solution)/shard_map/hkpn,hpki->kin/dot_general | solution.py:162
  116.2 3.3 %multiply_reduce_fusion = f32[2,256,256]{2,1,0:T(8,128)S(1)} fusion(f32[16,2,256]{2,1,0:T(2,128)S(1)} %copy.148, pred[256,256]{1,0:T(8,128)(4,1)S(1)} %copy-done.16, bf16[2,256,16,64]{1,0,3,2:T(2,128)(2,1)S(1)} %copy-done.10, bf16[16,64,2,256]{3,2,1,0:T(2,128)(2,1)S(1)} %copy-done.1), kind=kOutput, calls=%fused_computation.10 | convolution fusion | flops 278790144 | bytes 2719744 | tf_op jit(solution)/shard_map/hpki,kjhp->hkij/dot_general | solution.py:151
  119.5 0.8 copy-done.8
  120.3 1.1 convolution_add_fusion
  121.4 1.4 fusion.12
  122.9 52.3 %all-gather.5.cloned.1.call-done = f32[8,16,64,128]{3,2,1,0:T(8,128)} async-done(((f32[1,16,64,128]{3,2,1,0:T(8,128)}), f32[8,16,64,128]{3,2,1,0:T(8,128)}) %all-gather.5.cloned.1.call-update) | async-done | bytes 4194320 | tf_op jit(solution)/shard_map/all_gather | solution.py:14
  175.1 4.7 %rev.17 = f32[8,16,64,128]{3,2,1,0:T(8,128)} reverse(f32[8,16,64,128]{3,2,1,0:T(8,128)} %all-gather.5.cloned.1.call-done), dimensions={0} | reverse | bytes 8388608 | tf_op jit(solution)/shard_map/rev | solution.py:16
  179.9 8.7 %while.42 = (s32[]{:T(128)}, f32[16,64,128]{2,1,0:T(8,128)S(1)}, s32[]{:T(128)}, f32[8,16]{1,0:T(8,128)S(1)}, f32[8,16,64,128]{3,2,1,0:T(8,128)}, /*index=5*/s32[]{:T(128)}, s32[]{:T(128)}) while((s32[]{:T(128)}, f32[16,64,128]{2,1,0:T(8,128)S(1)}, s32[]{:T(128)}, f32[8,16]{1,0:T(8,128)S(1)}, f32[8,16,64,128]{3,2,1,0:T(8,128)}, ...), condition=%wide.region_4.5_spmd.clone, body=%wide.region_3.4_spmd.clone.sunk | while | flops 524292 | bytes 1573169 | solution.py:26
  179.9 1.2 fusion.68
  181.1 1.2 fusion.68
  182.3 1.2 fusion.68
  183.5 1.2 fusion.68
  184.7 1.2 fusion.68
  186.0 1.2 fusion.68
  187.2 1.2 fusion.68
  188.6 1.3 fusion.46
  189.9 1.0 fusion.34
  190.9 4.2 %fusion.27 = f32[2,256,128]{2,1,0:T(8,128)} fusion(f32[2,256,16]{1,2,0:T(8,128)S(1)} %bitcast.160, bf16[2,256,16,64]{1,0,3,2:T(2,128)(2,1)S(1)} %copy-done.11, f32[16,1,64,128]{3,2,0,1:T(8,128)S(1)} %bitcast.147, f32[16,1,64,128]{3,2,0,1:T(8,128)S(1)} %fusion.46), kind=kOutput, calls=%fused_computation.38 | convolution fusion | flops 806617088 | bytes 2392064 | tf_op jit(solution)/shard_map/hkpn,kjhp->kjn/dot_general | solution.py:176
  195.2 6.5 %fusion.10 = (f32[2,256,16]{1,2,0:T(8,128)S(1)}, bf16[2,256,16,64]{1,3,2,0:T(8,128)(2,1)}) fusion(bf16[2,256,16,64]{1,0,3,2:T(2,128)(2,1)S(1)} %copy-done.11, f32[2,256,16]{1,2,0:T(8,128)S(1)} %bitcast.161, f32[2,16,64,256]{3,2,1,0:T(8,128)S(1)} %fusion.34, bf16[16,64,2,256]{3,2,1,0:T(2,128)(2,1)S(1)} %copy-done.2, f32[2,256,256]{2,1,0:T(8,128)S(1)} %copy-done.14, ...), kind=kOutput, calls=%fused_computation.22 | convolution fusion | flops 1622138880 | bytes 5931008 | tf_op jit(solution)/shard_map/hkij,hpki->kjhp/dot_general | solution.py:133
  201.8 0.3 rev.18
  202.1 1.1 reduce-window.16
  203.5 0.3 rev.19
  203.8 0.2 slice_reduce_fusion.3
  204.0 3.9 %copy.176 = bf16[2,256,16,64]{3,2,1,0:T(8,128)(2,1)} copy(bf16[2,256,16,64]{1,3,2,0:T(8,128)(2,1)} %get-tuple-element.368) | data formatting | bytes 2097152
  207.9 4.1 %reshape.208 = bf16[512,1024]{1,0:T(8,128)(2,1)} reshape(bf16[2,256,16,64]{3,2,1,0:T(8,128)(2,1)} %copy.176) | data formatting | bytes 2097152
  211.9 1.6 convolution_add_fusion.1
  213.5 0.8 pad_maximum_fusion.4
  214.4 0.2 dynamic-update-slice.1
  214.6 18.8 %all-reduce.1 = f32[128]{0:T(128)S(1)} all-reduce(f32[128]{0:T(128)S(1)} %dynamic-update-slice.1), channel_id=3, replica_groups=mesh['grp'=2,'seq'=8,'head'=2] {'seq'}, use_global_device_ids=true, to_apply=%add.1 | all-reduce | flops 128 | bytes 1024
  233.6 0.3 while.44
  233.8 0.7 broadcast_add_fusion
  (96 shorter events, 1.7 us)
Async XLA Ops:
  8.0 1.6 copy-start
  8.0 20.7 %reduce-scatter.3.cloned.1.call-start = ((), (), s32[]{:S(2)}) async-start(), calls=%async_computation.2 | async-start | bytes 6291456 | tf_op jit(solution)/shard_map/reduce_scatter | solution.py:54
  13.8 2.7 %copy-start.18 = (f32[16,512]{1,0:T(8,128)S(1)}, f32[16,512]{1,0:T(8,128)}, u32[]{:S(2)}) copy-start(f32[16,512]{1,0:T(8,128)} %param.15) | copy-start | bytes 98308
  13.8 4.1 %copy-start.5 = (bf16[512,128]{1,0:T(8,128)(2,1)S(1)}, bf16[512,128]{1,0:T(8,128)(2,1)}, u32[]{:S(2)}) copy-start(bf16[512,128]{1,0:T(8,128)(2,1)} %param.13) | copy-start | bytes 393220
  13.8 4.6 %copy-start.19 = (u32[32]{0:T(128)S(1)}, u32[32]{0:T(128)}, u32[]{:S(2)}) copy-start(u32[32]{0:T(128)} %constant.88) | copy-start | bytes 388
  13.9 87.6 %all-gather.7.cloned.1.call-start = ((), (), s32[]{:S(2)}) async-start(), calls=%async_computation.4 | async-start | bytes 4718592 | tf_op jit(solution)/shard_map/all_gather | solution.py:14
  15.4 10.1 %copy-start.6 = (bf16[512,128]{1,0:T(8,128)(2,1)S(1)}, bf16[512,128]{1,0:T(8,128)(2,1)}, u32[]{:S(2)}) copy-start(bf16[512,128]{1,0:T(8,128)(2,1)} %param.14) | copy-start | bytes 393220
  23.4 1.1 copy-start.4
  25.4 149.7 %all-gather.5.cloned.1.call-start = ((), (), s32[]{:S(2)}) async-start(), calls=%async_computation.3 | async-start | bytes 4718592 | tf_op jit(solution)/shard_map/all_gather | solution.py:14
  35.1 1.0 copy-start.3
  37.1 197.5 %reduce-scatter.5.cloned.1.call-start = ((), (), s32[]{:S(2)}) async-start(), calls=%async_computation.5 | async-start | bytes 786432 | tf_op jit(solution)/shard_map/reduce_scatter | solution.py:186
  59.5 0.6 copy-start.15
  60.1 0.8 copy-start.13
  110.0 6.1 %copy-start.1 = (bf16[16,64,2,256]{3,2,1,0:T(2,128)(2,1)S(1)}, bf16[16,64,2,256]{3,2,1,0:T(2,128)(2,1)}, u32[]{:S(2)}) copy-start(bf16[16,64,2,256]{3,2,1,0:T(2,128)(2,1)} %reshape.180) | copy-start | bytes 3145732
  110.0 6.1 %copy-start.10 = (bf16[2,256,16,64]{1,0,3,2:T(2,128)(2,1)S(1)}, bf16[2,256,16,64]{1,0,3,2:T(2,128)(2,1)}, u32[]{:S(2)}) copy-start(bf16[2,256,16,64]{1,0,3,2:T(2,128)(2,1)} %reshape.186) | copy-start | bytes 3145732
  110.0 6.1 %copy-start.16 = (pred[256,256]{1,0:T(8,128)(4,1)S(1)}, pred[256,256]{1,0:T(8,128)(4,1)}, u32[]{:S(2)}) copy-start(pred[256,256]{1,0:T(8,128)(4,1)} %copy-done.15) | copy-start | bytes 196612
  116.1 5.3 %copy-start.7 = (f32[16,2,256,64]{2,3,1,0:T(8,128)S(1)}, f32[16,2,256,64]{2,3,1,0:T(8,128)}, u32[]{:S(2)}) copy-start(f32[16,2,256,64]{2,3,1,0:T(8,128)} %fusion.19) | copy-start | bytes 6291460
  119.5 0.8 copy-start.8
  188.6 2.4 copy-start.11
  188.6 6.6 %copy-start.2 = (bf16[16,64,2,256]{3,2,1,0:T(2,128)(2,1)S(1)}, bf16[16,64,2,256]{3,2,1,0:T(2,128)(2,1)}, u32[]{:S(2)}) copy-start(bf16[16,64,2,256]{3,2,1,0:T(2,128)(2,1)} %reshape.180) | copy-start | bytes 3145732
  188.6 6.6 %copy-start.14 = (f32[2,256,256]{2,1,0:T(8,128)S(1)}, f32[2,256,256]{2,1,0:T(8,128)}, u32[]{:S(2)}) copy-start(f32[2,256,256]{2,1,0:T(8,128)} %copy-done.13) | copy-start | bytes 1572868
  188.6 6.6 %copy-start.17 = (pred[256,256]{1,0:T(8,128)(4,1)S(1)}, pred[256,256]{1,0:T(8,128)(4,1)}, u32[]{:S(2)}) copy-start(pred[256,256]{1,0:T(8,128)(4,1)} %copy-done.15) | copy-start | bytes 196612
  201.7 10.2 %copy-start.9 = (f32[2,256,256]{2,1,0:T(8,128)S(1)}, f32[2,256,256]{2,1,0:T(8,128)}, u32[]{:S(2)}) copy-start(f32[2,256,256]{2,1,0:T(8,128)} %copy-done.8) | copy-start | bytes 1572868
  201.7 11.8 %copy-start.12 = (f32[2,256,128]{2,1,0:T(8,128)S(1)}, f32[2,256,128]{2,1,0:T(8,128)}, u32[]{:S(2)}) copy-start(f32[2,256,128]{2,1,0:T(8,128)} %convolution_add_fusion) | copy-start | bytes 786436
Sparse Core Ops, SparseCore 0:
  14.0 14.7 reduce-scatter.2
  214.5 6.3 reduce-scatter.4
Sparse Core Ops, SparseCore 1:
  25.5 75.9 all-gather.6
  103.7 71.4 all-gather.4
where the time goes:
time: 243 us; the launch traced here: 242 us
  waiting for transfers between devices  86.8 us (36%)
  matrix products  44 us (18%)
  blocking collectives  41.1 us (17%)
  other arithmetic  27.8 us (11%)
  local copies, waits for them, and re-layouts  24.7 us (10%)
  between operations  16.6 us (7%)
    all_gather x2, waiting for transfers between devices, entering(): pieces = jax.tree.map(lambda part: lax.all_gather(part, axis), value)  84.3 us
    unnamed x2, blocking collectives  41.1 us
    select_n x21, other arithmetic, lap(): jnp.where(position < mine, new, old)  16.6 us
    unnamed x48, local copies, waits for them, and re-layouts  15.9 us
    dot_general x1, matrix products, body(): jnp.einsum('hkij,kjhp->hpki', weights, feature_blocks, precision=blended,...  8.59 us
    dot_general x1, matrix products, body(): jnp.einsum('hkij,hpki->kjhp', weights, grad_output, precision=blended, pr...  6.52 us
  transfers between devices with their start and end apart: 4, of which 3 were waited for; matrix products, arithmetic and copies ran while one was open for 20% of the time, Pallas kernels for 0%

commit v1 on v0

v1 whole, which is shorter than its diff:
```python
import functools

import jax
import jax.numpy as jnp
from jax import lax
from jax.experimental import pallas as pl
from jax.experimental.pallas import tpu as pltpu
from jax.sharding import PartitionSpec as P

BLOCK = 256
F32 = jnp.float32
BF16 = jnp.bfloat16
MESH = pl.DeviceIdType.MESH


def nn(a, b, **kw):
    return lax.dot_general(a, b, (((1,), (0,)), ((), ())), preferred_element_type=F32, **kw)


def nt(a, b, **kw):
    return lax.dot_general(a, b, (((1,), (1,)), ((), ())), preferred_element_type=F32, **kw)


def tn(a, b, **kw):
    return lax.dot_general(a, b, (((0,), (0,)), ((), ())), preferred_element_type=F32, **kw)


def kernel(
    n, heads, hs, blocks,
    f_ref, k_ref, q_ref, ld_ref, w_ref, og_ref,
    gf_ref, gp_ref, gd_ref,
    w_in, og_in, gp_in, gp_stage, tot,
    stage, pair_in, half, z_in, ret_out, ret_in,
    a_ref, ac_ref, xt, xs, gt, gs, gi, fresh, up, local, enter, mis, mixsum, scm,
    hd_send, hd_recv, tot_send, tot_recv, pr_send, pr_recv, z_send, z_recv,
):
    me = lax.axis_index("seq")
    hd = lax.axis_index("head")
    other = 1 - hd
    pairs = n // 2
    pair = me // 2
    par = lax.rem(me, 2)
    mate = me + 1 - 2 * par
    inner = heads * hs
    hh = heads // 2
    hrows = inner // 2
    tokens = blocks * BLOCK

    barrier = pltpu.get_barrier_semaphore()
    pl.semaphore_signal(barrier, inc=1, device_id={"head": other}, device_id_type=MESH)

    def greet(j, c):
        @pl.when(j != me)
        def _():
            pl.semaphore_signal(barrier, inc=1, device_id={"seq": j}, device_id_type=MESH)
        return c

    lax.fori_loop(0, n, greet, 0)
    pl.semaphore_wait(barrier, n)

    def to_head(src, dst, i):
        return pltpu.make_async_remote_copy(
            src_ref=src, dst_ref=dst, send_sem=hd_send.at[i], recv_sem=hd_recv.at[i],
            device_id={"head": other}, device_id_type=MESH)

    send_og = to_head(og_ref, og_in, 0)
    send_w = to_head(w_ref.at[pl.ds(pl.multiple_of(other * inner, inner), inner), :], w_in, 1)
    send_og.start()
    send_w.start()

    rows = lax.broadcasted_iota(jnp.int32, (BLOCK, BLOCK), 0)
    cols = lax.broadcasted_iota(jnp.int32, (BLOCK, BLOCK), 1)
    upper = (rows <= cols).astype(F32)
    hi = lax.Precision.HIGHEST
    lasts = []
    for b in range(blocks):
        ld = ld_ref[:, b * BLOCK:(b + 1) * BLOCK]
        a = nn(ld, upper, precision=hi)
        at = lax.dot_general(upper, ld, (((0,), (1,)), ((), ())), preferred_element_type=F32, precision=hi)
        a_ref[b] = a
        for h in range(heads):
            ac_ref[b, h] = at[:, h:h + 1]
        lasts.append(jnp.broadcast_to(a[:, BLOCK - 1:BLOCK], (heads, 128)))
    total = lasts[0]
    for b in range(1, blocks):
        total = total + lasts[b]
    e = [jnp.exp(v) for v in lasts]
    tot[me] = total

    def tot_copy(j):
        return pltpu.make_async_remote_copy(
            src_ref=tot.at[me], dst_ref=tot.at[me], send_sem=tot_send.at[j], recv_sem=tot_recv.at[me],
            device_id={"seq": j}, device_id_type=MESH)

    def tot_go(j, c):
        @pl.when(j != me)
        def _():
            tot_copy(j).start()
        return c

    lax.fori_loop(0, n, tot_go, 0)

    for b in range(blocks):
        xt[b] = f_ref[b * BLOCK:(b + 1) * BLOCK, :].T
        for h in range(heads):
            r = slice(h * hs, (h + 1) * hs)
            arow = a_ref[b, h:h + 1, :]
            tail = jnp.exp(arow[:, BLOCK - 1:BLOCK] - arow)
            xs[b, r, :] = (xt[b, r, :].astype(F32) * tail).astype(BF16)
        fresh[b] = nn(xs[b], k_ref[b * BLOCK:(b + 1) * BLOCK, :])
    for h in range(heads):
        r = slice(h * hs, (h + 1) * hs)
        s = fresh[0, r, :]
        for b in range(1, blocks):
            s = e[b][h:h + 1, :] * s + fresh[b, r, :]
        local[0, r, :] = s
        stage[0, r, :] = s.astype(BF16)

    mine_rows = pl.ds(pl.multiple_of(par * hrows, hrows), hrows)
    mate_rows = pl.ds(pl.multiple_of((1 - par) * hrows, hrows), hrows)

    def to_mate(src, dst, i):
        return pltpu.make_async_remote_copy(
            src_ref=src, dst_ref=dst, send_sem=pr_send.at[i], recv_sem=pr_recv.at[i],
            device_id={"seq": mate}, device_id_type=MESH)

    pair_f = to_mate(stage.at[0, mate_rows, :], pair_in.at[0], 0)
    pair_f.start()

    for b in range(blocks):
        t = slice(b * BLOCK, (b + 1) * BLOCK)
        scm[b] = jnp.where(rows >= cols, nt(q_ref[t, :], k_ref[t, :]), 0.0)
        mixsum[b] = jnp.zeros((BLOCK, BLOCK), F32)

    send_og.wait_recv()
    send_w.wait_recv()
    chunk = 8 * hs

    def g_step(i, c):
        r0 = pl.multiple_of(i * chunk, chunk)
        w_own = w_ref[pl.ds(pl.multiple_of(hd * inner + r0, chunk), chunk), :]
        g = nt(w_own, og_ref[...]) + nt(w_in[pl.ds(r0, chunk), :], og_in[...])
        g = g.astype(BF16)
        for b in range(blocks):
            gb = g[:, b * BLOCK:(b + 1) * BLOCK]
            gt[b, pl.ds(r0, chunk), :] = gb
            growth = jnp.exp(a_ref[b, pl.ds(pl.multiple_of(i * 8, 8), 8), :])
            for m in range(8):
                gs[b, pl.ds(pl.multiple_of(r0 + m * hs, hs), hs), :] = (
                    gb[m * hs:(m + 1) * hs, :].astype(F32) * growth[m:m + 1, :]).astype(BF16)
        return c

    lax.fori_loop(0, heads // 8, g_step, 0)
    for b in range(blocks):
        up[b] = nn(gs[b], q_ref[b * BLOCK:(b + 1) * BLOCK, :])
    for h in range(heads):
        r = slice(h * hs, (h + 1) * hs)
        s = up[blocks - 1, r, :]
        for b in reversed(range(blocks - 1)):
            s = e[b][h:h + 1, :] * s + up[b, r, :]
        local[1, r, :] = s
        stage[1, r, :] = s.astype(BF16)
    pair_b = to_mate(stage.at[1, mate_rows, :], pair_in.at[1], 1)
    pair_b.start()

    def tot_wait(j, c):
        @pl.when(j != me)
        def _():
            pltpu.make_async_remote_copy(
                src_ref=tot.at[j], dst_ref=tot.at[j], send_sem=tot_send.at[j], recv_sem=tot_recv.at[j],
                device_id={"seq": j}, device_id_type=MESH).wait_recv()
        return c

    lax.fori_loop(0, n, tot_wait, 0)
    e_lo = jnp.exp(tot[2 * pair, pl.ds(pl.multiple_of(par * hh, hh), hh), :])
    e_hi = jnp.exp(tot[2 * pair + 1, pl.ds(pl.multiple_of(par * hh, hh), hh), :])
    is_lo = par == 0

    def z_copy(d, zz):
        return pltpu.make_async_remote_copy(
            src_ref=half.at[d], dst_ref=z_in.at[d, pair],
            send_sem=z_send.at[d, zz], recv_sem=z_recv.at[d, pair],
            device_id={"seq": 2 * zz + par}, device_id_type=MESH)

    def sides(d, h):
        own = local[d, pl.ds(pl.multiple_of(par * hrows + h * hs, hs), hs), :]
        got = pair_in[d, h * hs:(h + 1) * hs, :].astype(F32)
        return jnp.where(is_lo, own, got), jnp.where(is_lo, got, own)

    pair_f.wait_recv()
    for h in range(hh):
        lo, high = sides(0, h)
        half[0, h * hs:(h + 1) * hs, :] = (e_hi[h:h + 1, :] * lo + high).astype(BF16)

    def z_go(d, zz):
        @pl.when(zz > pair if d == 0 else zz < pair)
        def _():
            z_copy(d, zz).start()

    def z_each(d, act):
        def run(zz, c):
            @pl.when(zz > pair if d == 0 else zz < pair)
            def _():
                act(z_copy(d, zz))
            return c
        lax.fori_loop(0, pairs, run, 0)

    z_each(0, lambda c: c.start())
    pair_b.wait_recv()
    for h in range(hh):
        lo, high = sides(1, h)
        half[1, h * hs:(h + 1) * hs, :] = (e_lo[h:h + 1, :] * high + lo).astype(BF16)
    z_each(1, lambda c: c.start())

    def head_step(h, c):
        r = pl.ds(pl.multiple_of(h * hs, hs), hs)
        for b in range(blocks):
            gap = jnp.minimum(ac_ref[b, h] - a_ref[b, pl.ds(h, 1), :], 0.0)
            within = jnp.exp(gap)
            gh = gt[b, r, :]
            xh = xt[b, r, :]
            mixsum[b] += within * tn(gh, xh)
            weights = (within * scm[b]).astype(BF16)
            y = nt(xh, weights)
            gin = nn(gh, weights)
            gi[b, r, :] = gin
            mis[b, pl.ds(h, 1), :] = jnp.sum(gh.astype(F32) * y - xh.astype(F32) * gin, axis=0, keepdims=True)
        return c

    lax.fori_loop(0, heads, head_step, 0)

    enter[:, mine_rows, :] = jnp.zeros((2, hrows, 128), F32)
    half_heads = pl.ds(pl.multiple_of(par * hh, hh), hh)
    for d in range(2):
        def gather(step, c, d=d):
            zz = step if d == 0 else pairs - 1 - step

            @pl.when(zz < pair if d == 0 else zz > pair)
            def _():
                pltpu.make_async_remote_copy(
                    src_ref=half.at[d], dst_ref=z_in.at[d, zz],
                    send_sem=z_send.at[d, zz], recv_sem=z_recv.at[d, zz],
                    device_id={"seq": 2 * zz + par}, device_id_type=MESH).wait_recv()
                ez = jnp.exp(tot[2 * zz, half_heads, :] + tot[2 * zz + 1, half_heads, :])
                for h in range(hh):
                    r = pl.ds(pl.multiple_of(par * hrows + h * hs, hs), hs)
                    enter[d, r, :] = ez[h:h + 1, :] * enter[d, r, :] + z_in[d, zz, h * hs:(h + 1) * hs, :].astype(F32)
            return c

        lax.fori_loop(0, pairs, gather, 0)
    rets = []
    for d in range(2):
        for h in range(hh):
            r = pl.ds(pl.multiple_of(par * hrows + h * hs, hs), hs)
            lo, high = sides(d, h)
            base = enter[d, r, :]
            if d == 0:
                far = e_lo[h:h + 1, :] * base + lo
                far_mine = par == 1
            else:
                far = e_hi[h:h + 1, :] * base + high
                far_mine = par == 0
            enter[d, r, :] = jnp.where(far_mine, far, base)
            ret_out[d, h * hs:(h + 1) * hs, :] = jnp.where(far_mine, base, far).astype(BF16)
        c = to_mate(ret_out.at[d], ret_in.at[d], 2 + d)
        c.start()
        rets.append(c)
    for d in range(2):
        rets[d].wait_recv()
        enter[d, mate_rows, :] = ret_in[d].astype(F32)

    for h in range(heads):
        r = slice(h * hs, (h + 1) * hs)
        states = [enter[0, r, :]]
        for b in range(blocks):
            states.append(e[b][h:h + 1, :] * states[b] + fresh[b, r, :])
        adj = enter[1, r, :]
        for b in reversed(range(blocks)):
            nxt = e[b][h:h + 1, :] * adj + up[b, r, :]
            base = jnp.sum(jnp.sum(states[b + 1] * adj, axis=0, keepdims=True), axis=1, keepdims=True)
            gd_ref[h:h + 1, b * BLOCK:(b + 1) * BLOCK] = jnp.broadcast_to(base, (1, BLOCK))
            up[b, r, :] = adj
            adj = nxt
        for b in range(blocks):
            fresh[b, r, :] = states[b]
    lower = (rows >= cols).astype(F32)
    for b in range(blocks):
        t = slice(b * BLOCK, (b + 1) * BLOCK)
        kb = k_ref[t, :]
        qb = q_ref[t, :]
        sb = fresh[b].astype(BF16)
        ab = up[b].astype(BF16)
        mixed = jnp.where(rows >= cols, mixsum[b], 0.0).astype(BF16)
        gp_stage[0, t, :] = tn(mixed, qb) + tn(xs[b], ab)
        gp_stage[1, t, :] = nn(mixed, kb) + tn(gs[b], sb)
    send_gp = to_head(gp_stage.at[other], gp_in, 2)
    send_gp.start()
    for b in range(blocks):
        t = slice(b * BLOCK, (b + 1) * BLOCK)
        kb = k_ref[t, :]
        qb = q_ref[t, :]
        for h in range(heads):
            r = slice(h * hs, (h + 1) * hs)
            arow = a_ref[b, h:h + 1, :]
            tail = jnp.exp(arow[:, BLOCK - 1:BLOCK] - arow)
            growth = jnp.exp(arow)
            yc = nt(fresh[b, r, :].astype(BF16), qb)
            gc = nt(up[b, r, :].astype(BF16), kb) * tail
            gi[b, r, :] += gc
            mis[b, h:h + 1, :] += (
                jnp.sum(gt[b, r, :].astype(F32) * yc, axis=0, keepdims=True) * growth
                - jnp.sum(xt[b, r, :].astype(F32) * gc, axis=0, keepdims=True))
        gf_ref[t, :] = gi[b].astype(BF16).T
        gd_ref[:, t] += nn(mis[b], lower, precision=hi)
    send_gp.wait_recv()
    gp_ref[0] = gp_stage[hd] + gp_in[...]

    send_og.wait_send()
    send_w.wait_send()
    send_gp.wait_send()
    pair_f.wait_send()
    pair_b.wait_send()
    for d in range(2):
        rets[d].wait_send()
        z_each(d, lambda c: c.wait_send())

    def tot_done(j, c):
        @pl.when(j != me)
        def _():
            tot_copy(j).wait_send()
        return c

    lax.fori_loop(0, n, tot_done, 0)


def body(n, features, keys_proj, query_proj, log_decay, out_weight, out_grad):
    tokens, inner = features.shape
    heads = log_decay.shape[0]
    hs = inner // heads
    ns = keys_proj.shape[1]
    depth = out_grad.shape[1]
    blocks = tokens // BLOCK
    pairs = n // 2
    half = inner // 2
    vm = pltpu.VMEM
    dma = pltpu.SemaphoreType.DMA
    scratch = [
        vm((inner, depth), BF16), vm((tokens, depth), BF16), vm((tokens, ns), F32),
        vm((2, tokens, ns), F32), vm((n, heads, 128), F32),
        vm((2, inner, ns), BF16), vm((2, half, ns), BF16), vm((2, half, ns), BF16),
        vm((2, pairs, half, ns), BF16), vm((2, half, ns), BF16), vm((2, half, ns), BF16),
        vm((blocks, heads, BLOCK), F32), vm((blocks, heads, BLOCK, 1), F32),
        vm((blocks, inner, BLOCK), BF16), vm((blocks, inner, BLOCK), BF16),
        vm((blocks, inner, BLOCK), BF16), vm((blocks, inner, BLOCK), BF16),
        vm((blocks, inner, BLOCK), F32),
        vm((blocks, inner, ns), F32), vm((blocks, inner, ns), F32),
        vm((2, inner, ns), F32), vm((2, inner, ns), F32),
        vm((blocks, heads, BLOCK), F32), vm((blocks, BLOCK, BLOCK), F32), vm((blocks, BLOCK, BLOCK), F32),
        dma((3,)), dma((3,)), dma((n,)), dma((n,)), dma((4,)), dma((4,)),
        dma((2, pairs)), dma((2, pairs)),
    ]
    spec = pl.BlockSpec(memory_space=pltpu.VMEM)
    return pl.pallas_call(
        functools.partial(kernel, n, heads, hs, blocks),
        out_shape=(
            jax.ShapeDtypeStruct((tokens, inner), BF16),
            jax.ShapeDtypeStruct((1, tokens, ns), F32),
            jax.ShapeDtypeStruct((heads, tokens), F32),
        ),
        in_specs=[spec] * 6,
        out_specs=(spec,) * 3,
        scratch_shapes=scratch,
        compiler_params=pltpu.CompilerParams(
            collective_id=0, has_side_effects=True, vmem_limit_bytes=56 * 1024 * 1024),
    )(features, keys_proj, query_proj, log_decay, out_weight, out_grad)


def solution(mesh):
    placed = (
        P(("grp", "seq"), "head"),
        P(("grp", "seq"), None),
        P(("grp", "seq"), None),
        P("head", ("grp", "seq")),
        P(None, "head"),
        P(("grp", "seq"), "head"),
    )
    return jax.shard_map(
        functools.partial(body, mesh.shape["seq"]),
        mesh=mesh,
        in_specs=placed,
        out_specs=(
            P(("grp", "seq"), "head"),
            P("head", ("grp", "seq"), None),
            P("head", ("grp", "seq")),
        ),
        check_vma=False,
    )
```

time: 243 us -> 45.1 us (0.19)
  waiting for transfers between devices: 86.8 us -> 0 us
  matrix products: 44 us -> 0 us
  blocking collectives: 41.1 us -> 0 us
  Pallas kernels: 0 us -> 40.4 us
  other arithmetic: 27.8 us -> 0 us
  local copies, waits for them, and re-layouts: 24.7 us -> 3.63 us
  between operations: 16.6 us -> 0.66 us
    all_gather x2 -> x0, waiting for transfers between devices: 84.3 us -> none  [entering(): pieces = jax.tree.map(lambda part: lax.all_gather(part, axis), value)]
    dot_general x13 -> x0, matrix products: 44 us -> none  [the longest x1 8.59 us: body(): jnp.einsum('hkij,kjhp->hpki', weights, feature_blocks, precision=blended,...]
    unnamed x2 -> x0, blocking collectives: 41.1 us -> none
    pallas_call x0 -> x1, Pallas kernels: none -> 40.4 us  [body(): pl.pallas_call(functools.partial(kernel, n, heads, hs, blocks), out_shape...]
    select_n x21 -> x0, other arithmetic: 16.6 us -> none  [lap(): jnp.where(position < mine, new, old)]
    unnamed x48 -> x7, local copies, waits for them, and re-layouts: 15.9 us -> 3.63 us
    another operation x9 -> x0, other arithmetic: 5.97 us -> none
    rev x5 -> x0, local copies, waits for them, and re-layouts: 5.39 us -> none  [the longest x3 4.77 us: entering(): pieces = jax.tree.map(lambda part: part[::-1], pieces)]
  transfers between devices with their start and end apart: 4 -> 0, of which waited for: 3 -> 0; matrix products, arithmetic and copies ran while one was open for 20% -> 0% of each run, Pallas kernels for 0% -> 0%
where the time goes in v1:
time: 45.1 us; the launch traced here: 44.6 us
  Pallas kernels  40.4 us (90%)
  local copies, waits for them, and re-layouts  3.63 us (8%)
  between operations  0.66 us (1%)
    pallas_call x1, Pallas kernels, body(): pl.pallas_call(functools.partial(kernel, n, heads, hs, blocks), out_shape...  40.4 us
    unnamed x7, local copies, waits for them, and re-layouts  3.63 us

profile of v1, /device:TPU:0, one launch (start us, length us, event | category | flops | bytes accessed | tf_op | source)
XLA Modules:
  0.0 44.6 jit_solution(11622287676167124926)
XLA Ops:
  0.6 40.4 %shard_map.85 = (bf16[512,1024]{1,0:T(8,128)(2,1)}, f32[1,512,128]{2,1,0:T(8,128)}, f32[16,512]{1,0:T(8,128)}) custom-call(bf16[512,1024]{1,0:T(8,128)(2,1)} %f_ref.1, bf16[512,128]{1,0:T(8,128)(2,1)} %k_ref.1, bf16[512,128]{1,0:T(8,128)(2,1)} %q_ref.1, f32[16,512]{1,0:T(8,128)} %ld_ref.1, bf16[2048,512]{1,0:T(8,128)(2,1)} %w_ref.1, bf16[512,512]{1,0:T(8,128)(2,1)} %og_ref.1), custom_call_target="tpu_custom_call" | custom-call | tf_op jit(solution)/shard_map/pallas_call | solution.py:363
  41.0 0.0 copy-start
  41.0 0.0 copy-start.1
  41.0 2.3 %copy.12 = bf16[512,1024]{1,0:T(8,128)(2,1)} copy(bf16[512,1024]{1,0:T(8,128)(2,1)} %get-tuple-element.6) | data formatting | bytes 2097152
  43.3 0.0 copy-done
  43.3 0.7 %copy.13 = f32[1,512,128]{2,1,0:T(8,128)} copy(f32[1,512,128]{2,1,0:T(8,128)S(1)} %copy-done) | data formatting | bytes 524288
  44.0 0.0 copy-done.1
  44.0 0.6 %copy.14 = f32[16,512]{1,0:T(8,128)} copy(f32[16,512]{1,0:T(8,128)S(1)} %copy-done.1) | data formatting | bytes 65536
Async XLA Ops:
  41.0 2.3 %copy-start = (f32[1,512,128]{2,1,0:T(8,128)S(1)}, f32[1,512,128]{2,1,0:T(8,128)}, u32[]{:S(2)}) copy-start(f32[1,512,128]{2,1,0:T(8,128)} %get-tuple-element.7) | copy-start | bytes 786436
  41.0 3.0 %copy-start.1 = (f32[16,512]{1,0:T(8,128)S(1)}, f32[16,512]{1,0:T(8,128)}, u32[]{:S(2)}) copy-start(f32[16,512]{1,0:T(8,128)} %get-tuple-element.8) | copy-start | bytes 98308

commit v2 on v1

--- a/solution.py
+++ b/solution.py
@@ -76,10 +76,7 @@
     for b in range(blocks):
         ld = ld_ref[:, b * BLOCK:(b + 1) * BLOCK]
         a = nn(ld, upper, precision=hi)
-        at = lax.dot_general(upper, ld, (((0,), (1,)), ((), ())), preferred_element_type=F32, precision=hi)
         a_ref[b] = a
-        for h in range(heads):
-            ac_ref[b, h] = at[:, h:h + 1]
         lasts.append(jnp.broadcast_to(a[:, BLOCK - 1:BLOCK], (heads, 128)))
     total = lasts[0]
     for b in range(1, blocks):
@@ -127,11 +124,6 @@
     pair_f = to_mate(stage.at[0, mate_rows, :], pair_in.at[0], 0)
     pair_f.start()
 
-    for b in range(blocks):
-        t = slice(b * BLOCK, (b + 1) * BLOCK)
-        scm[b] = jnp.where(rows >= cols, nt(q_ref[t, :], k_ref[t, :]), 0.0)
-        mixsum[b] = jnp.zeros((BLOCK, BLOCK), F32)
-
     send_og.wait_recv()
     send_w.wait_recv()
     chunk = 8 * hs
@@ -206,6 +198,15 @@
         lax.fori_loop(0, pairs, run, 0)
 
     z_each(0, lambda c: c.start())
+
+    for b in range(blocks):
+        t = slice(b * BLOCK, (b + 1) * BLOCK)
+        scm[b] = jnp.where(rows >= cols, nt(q_ref[t, :], k_ref[t, :]), 0.0)
+        mixsum[b] = jnp.zeros((BLOCK, BLOCK), F32)
+        at = lax.dot_general(upper, ld_ref[:, t], (((0,), (1,)), ((), ())), preferred_element_type=F32, precision=hi)
+        for h in range(heads):
+            ac_ref[b, h] = at[:, h:h + 1]
+
     pair_b.wait_recv()
     for h in range(hh):
         lo, high = sides(1, h)
@@ -231,6 +232,7 @@
 
     enter[:, mine_rows, :] = jnp.zeros((2, hrows, 128), F32)
     half_heads = pl.ds(pl.multiple_of(par * hh, hh), hh)
+    rets = []
     for d in range(2):
         def gather(step, c, d=d):
             zz = step if d == 0 else pairs - 1 - step
@@ -248,8 +250,6 @@
             return c
 
         lax.fori_loop(0, pairs, gather, 0)
-    rets = []
-    for d in range(2):
         for h in range(hh):
             r = pl.ds(pl.multiple_of(par * hrows + h * hs, hs), hs)
             lo, high = sides(d, h)
@@ -265,51 +265,57 @@
         c = to_mate(ret_out.at[d], ret_in.at[d], 2 + d)
         c.start()
         rets.append(c)
-    for d in range(2):
-        rets[d].wait_recv()
-        enter[d, mate_rows, :] = ret_in[d].astype(F32)
-
+    rets[0].wait_recv()
+    enter[0, mate_rows, :] = ret_in[0].astype(F32)
     for h in range(heads):
         r = slice(h * hs, (h + 1) * hs)
-        states = [enter[0, r, :]]
+        state = enter[0, r, :]
         for b in range(blocks):
-            states.append(e[b][h:h + 1, :] * states[b] + fresh[b, r, :])
+            nxt = e[b][h:h + 1, :] * state + fresh[b, r, :]
+            fresh[b, r, :] = state
+            state = nxt
+        local[0, r, :] = state
+    for b in range(blocks):
+        t = slice(b * BLOCK, (b + 1) * BLOCK)
+        qb = q_ref[t, :]
+        sb = fresh[b].astype(BF16)
+        mixed = jnp.where(rows >= cols, mixsum[b], 0.0).astype(BF16)
+        gp_stage[0, t, :] = tn(mixed, qb)
+        gp_stage[1, t, :] = nn(mixed, k_ref[t, :]) + tn(gs[b], sb)
+        for h in range(heads):
+            r = slice(h * hs, (h + 1) * hs)
+            growth = jnp.exp(a_ref[b, h:h + 1, :])
+            yc = nt(sb[r, :], qb)
+            mis[b, h:h + 1, :] += jnp.sum(gt[b, r, :].astype(F32) * yc, axis=0, keepdims=True) * growth
+
+    rets[1].wait_recv()
+    enter[1, mate_rows, :] = ret_in[1].astype(F32)
+    for h in range(heads):
+        r = slice(h * hs, (h + 1) * hs)
         adj = enter[1, r, :]
         for b in reversed(range(blocks)):
+            after = local[0, r, :] if b == blocks - 1 else fresh[b + 1, r, :]
             nxt = e[b][h:h + 1, :] * adj + up[b, r, :]
-            base = jnp.sum(jnp.sum(states[b + 1] * adj, axis=0, keepdims=True), axis=1, keepdims=True)
+            base = jnp.sum(jnp.sum(after * adj, axis=0, keepdims=True), axis=1, keepdims=True)
             gd_ref[h:h + 1, b * BLOCK:(b + 1) * BLOCK] = jnp.broadcast_to(base, (1, BLOCK))
             up[b, r, :] = adj
             adj = nxt
-        for b in range(blocks):
-            fresh[b, r, :] = states[b]
     lower = (rows >= cols).astype(F32)
+    for b in range(blocks):
+        t = slice(b * BLOCK, (b + 1) * BLOCK)
+        gp_stage[0, t, :] += tn(xs[b], up[b].astype(BF16))
+    send_gp = to_head(gp_stage.at[other], gp_in, 2)
+    send_gp.start()
     for b in range(blocks):
         t = slice(b * BLOCK, (b + 1) * BLOCK)
         kb = k_ref[t, :]
-        qb = q_ref[t, :]
-        sb = fresh[b].astype(BF16)
-        ab = up[b].astype(BF16)
-        mixed = jnp.where(rows >= cols, mixsum[b], 0.0).astype(BF16)
-        gp_stage[0, t, :] = tn(mixed, qb) + tn(xs[b], ab)
-        gp_stage[1, t, :] = nn(mixed, kb) + tn(gs[b], sb)
-    send_gp = to_head(gp_stage.at[other], gp_in, 2)
-    send_gp.start()
-    for b in range(blocks):
-        t = slice(b * BLOCK, (b + 1) * BLOCK)
-        kb = k_ref[t, :]
-        qb = q_ref[t, :]
         for h in range(heads):
             r = slice(h * hs, (h + 1) * hs)
             arow = a_ref[b, h:h + 1, :]
             tail = jnp.exp(arow[:, BLOCK - 1:BLOCK] - arow)
-            growth = jnp.exp(arow)
-            yc = nt(fresh[b, r, :].astype(BF16), qb)
             gc = nt(up[b, r, :].astype(BF16), kb) * tail
             gi[b, r, :] += gc
-            mis[b, h:h + 1, :] += (
-                jnp.sum(gt[b, r, :].astype(F32) * yc, axis=0, keepdims=True) * growth
-                - jnp.sum(xt[b, r, :].astype(F32) * gc, axis=0, keepdims=True))
+            mis[b, h:h + 1, :] -= jnp.sum(xt[b, r, :].astype(F32) * gc, axis=0, keepdims=True)
         gf_ref[t, :] = gi[b].astype(BF16).T
         gd_ref[:, t] += nn(mis[b], lower, precision=hi)
     send_gp.wait_recv()

time: 45.1 us -> 41.5 us (0.920)
  the two profiles are of different devices: /device:TPU:0 before, /device:TPU:9 now
where the time goes in v2:
time: 41.5 us; the launch traced here: 41.3 us
  Pallas kernels  37 us (89%)
  local copies, waits for them, and re-layouts  3.63 us (9%)
  between operations  0.66 us (2%)
    pallas_call x1, Pallas kernels, body(): pl.pallas_call(functools.partial(kernel, n, heads, hs, blocks), out_shape...  37 us
    unnamed x7, local copies, waits for them, and re-layouts  3.63 us

profile of v2, /device:TPU:9, one launch (start us, length us, event | category | flops | bytes accessed | tf_op | source)
XLA Modules:
  0.0 41.3 jit_solution(8661469159992522400)
XLA Ops:
  0.6 37.0 %shard_map.85 = (bf16[512,1024]{1,0:T(8,128)(2,1)}, f32[1,512,128]{2,1,0:T(8,128)}, f32[16,512]{1,0:T(8,128)}) custom-call(bf16[512,1024]{1,0:T(8,128)(2,1)} %f_ref.1, bf16[512,128]{1,0:T(8,128)(2,1)} %k_ref.1, bf16[512,128]{1,0:T(8,128)(2,1)} %q_ref.1, f32[16,512]{1,0:T(8,128)} %ld_ref.1, bf16[2048,512]{1,0:T(8,128)(2,1)} %w_ref.1, bf16[512,512]{1,0:T(8,128)(2,1)} %og_ref.1), custom_call_target="tpu_custom_call" | custom-call | tf_op jit(solution)/shard_map/pallas_call | solution.py:369
  37.7 0.0 copy-start
  37.7 0.0 copy-start.1
  37.7 2.3 %copy.12 = bf16[512,1024]{1,0:T(8,128)(2,1)} copy(bf16[512,1024]{1,0:T(8,128)(2,1)} %get-tuple-element.6) | data formatting | bytes 2097152
  40.0 0.0 copy-done
  40.0 0.7 %copy.13 = f32[1,512,128]{2,1,0:T(8,128)} copy(f32[1,512,128]{2,1,0:T(8,128)S(1)} %copy-done) | data formatting | bytes 524288
  40.7 0.0 copy-done.1
  40.7 0.6 %copy.14 = f32[16,512]{1,0:T(8,128)} copy(f32[16,512]{1,0:T(8,128)S(1)} %copy-done.1) | data formatting | bytes 65536
Async XLA Ops:
  37.7 2.3 %copy-start = (f32[1,512,128]{2,1,0:T(8,128)S(1)}, f32[1,512,128]{2,1,0:T(8,128)}, u32[]{:S(2)}) copy-start(f32[1,512,128]{2,1,0:T(8,128)} %get-tuple-element.7) | copy-start | bytes 786436
  37.7 3.0 %copy-start.1 = (f32[16,512]{1,0:T(8,128)S(1)}, f32[16,512]{1,0:T(8,128)}, u32[]{:S(2)}) copy-start(f32[16,512]{1,0:T(8,128)} %get-tuple-element.8) | copy-start | bytes 98308
